TPU v7x, 32 devices: a whole 2x2x4 slice. The times are simulated.
32 devices in a mesh: row: 4 (over y, core), col: 8 (over z, x).
Axes of the slice: x: 2, y: 2, z: 4, core: 2. Of those that a mesh axis runs over, the one named last changes fastest.
Arguments:
- shot_boxes: int32 [4, 4, 8192], P(None, 'row', 'col'), may hold values from 0 to 512, as said below
- block_counts: int32 [4, 8], P('row'), may hold values from 1 to 8, 32 in all within a row
- tail_shots: int32 [4, 8], P('row'), may hold values from 1 to 128
- doses: float32 [4, 8192], P('row', 'col'), may hold values from 0.5 to 1.5
- pixel_gain: float32 [2048, 4096], P('row', 'col'), may hold values from 0.6 to 1.6
Outputs:
- corrected: float32 [4, 8192], P('row', 'col')
- exposure: float32 [4, 8192], P('row', 'col')
Inputs may be any that keep to these rules, and one draw needn't show every extreme that they name: `shot_boxes`: every shot has 8 <= x1 - x0 <= 64 and 8 <= y1 - y0 <= 64, inside its tile of 512 pixels. `block_counts`: in every tile row the block counts sum to exactly 32, and some tile of the row has 8.
All inputs are finite; a program needn't handle non-finite values.
Results may differ from a plain program's by a relative error of at most 0.0003.
Values sent between devices are 32-bit elements; how exact they have to be, the bound alone decides.
A program may use at most 64 MiB of HBM per device.

v0:
```python
import math

import jax
import jax.numpy as jnp
from jax import lax
from jax.sharding import PartitionSpec as P

TILE = 512
CG = 128
BLK = 128
ITERS = 3
CELL = 4
BETA = 16
REACH = 32


FORWARD_RANGE = 4.0
BACK_RATIO = 0.75
TARGET_LEVEL = 1.0
EXACT_MODE = lax.Precision.HIGHEST


def with_halo(block, sides, width):
    for axis, dim in sides:
        count = lax.axis_size(axis)
        forward = [(i, i + 1) for i in range(count - 1)]
        backward = [(target, source) for source, target in forward]
        low = lax.ppermute(
            lax.slice_in_dim(block, block.shape[dim] - width, None, axis=dim), axis, forward
        )
        high = lax.ppermute(lax.slice_in_dim(block, 0, width, axis=dim), axis, backward)
        block = jnp.concatenate([low, block, high], axis=dim)
    return block


def edge_term(doubled, low_edge, high_edge):
    middle = doubled.astype(jnp.float32)[None, :] * 0.5
    low_side = low_edge.astype(jnp.float32)[:, None]
    high_side = high_edge.astype(jnp.float32)[:, None]
    return 0.5 * (
        jax.scipy.special.erf((middle - low_side) / FORWARD_RANGE)
        - jax.scipy.special.erf((middle - high_side) / FORWARD_RANGE)
    )


def pair_kernel(sources, centres):
    return edge_term(centres[0], sources[0], sources[2]) * edge_term(
        centres[1], sources[1], sources[3]
    )


def intersection(low_edge, high_edge):
    cell_edges = jnp.arange(CG, dtype=jnp.int32) * CELL
    covered = jnp.minimum(high_edge[:, None], cell_edges[None, :] + CELL) - jnp.maximum(
        low_edge[:, None], cell_edges[None, :]
    )
    return jnp.maximum(covered, 0).astype(jnp.float32) / CELL


def spread(distance):
    scaled = distance.astype(jnp.float32) / BETA
    inside = jnp.abs(distance) <= REACH
    return jnp.where(inside, jnp.exp(-scaled * scaled) / (math.sqrt(math.pi) * BETA), 0.0)


def body(shot_boxes, block_counts, tail_shots, doses, pixel_gain):
    shot_box = shot_boxes[:, 0, :]
    slot_count = shot_box.shape[1]
    col_count = lax.axis_size("col")
    col_index = lax.axis_index("col")
    peer_ids = jnp.arange(col_count, dtype=jnp.int32)
    blocks_row = block_counts[0]
    totals = (blocks_row - 1) * BLK + tail_shots[0]
    my_total = jnp.sum(jnp.where(peer_ids == col_index, totals, 0))
    is_live = jnp.arange(slot_count, dtype=jnp.int32) < my_total
    shot_dose = jnp.where(is_live, doses[0], 0.0)
    centres = jnp.stack([shot_box[0] + shot_box[2], shot_box[1] + shot_box[3]])
    cell_ids = centres[1] // (2 * CELL) * CG + centres[0] // (2 * CELL)
    pixel_ids = centres[1] // 2 * TILE + centres[0] // 2
    sensitive = pixel_gain.reshape(-1)[pixel_ids]
    across = intersection(shot_box[0], shot_box[2])
    downward = intersection(shot_box[1], shot_box[3])
    kernel = pair_kernel(shot_box, centres)
    local_cells = jnp.arange(CG, dtype=jnp.int32)
    padded_cells = jnp.arange(CG + 2 * REACH, dtype=jnp.int32)
    band_weights = spread(local_cells[:, None] + REACH - padded_cells[None, :])
    exposure = jnp.zeros_like(shot_dose)
    for sweep in range(ITERS):
        forward = jnp.dot(shot_dose, kernel, precision=EXACT_MODE)
        coarse = jnp.dot(downward.T, shot_dose[:, None] * across, precision=EXACT_MODE)
        widened = with_halo(coarse, (("row", 0), ("col", 1)), REACH)
        blurred = jnp.dot(band_weights, widened, precision=EXACT_MODE)
        background = jnp.dot(blurred, band_weights.T, precision=EXACT_MODE)
        sampled = background.reshape(-1)[cell_ids]
        exposure = sensitive * (forward + BACK_RATIO * sampled) / (1.0 + BACK_RATIO)
        shot_dose = jnp.where(
            is_live, shot_dose * TARGET_LEVEL / jnp.where(is_live, exposure, 1.0), 0.0
        )
    return (shot_dose[None, :], jnp.where(is_live, exposure, 0.0)[None, :])


def solution(mesh):
    placed = (
        P(None, "row", "col"),
        P("row", None),
        P("row", None),
        P("row", "col"),
        P("row", "col"),
    )
    return jax.shard_map(
        body,
        mesh=mesh,
        in_specs=placed,
        out_specs=(P("row", "col"), P("row", "col")),
        check_vma=False,
    )
```

profile of v0, /device:TPU:6, one launch (start us, length us, event | category | flops | bytes accessed | tf_op | source)
XLA Modules:
  0.0 93.2 jit_solution(5125635217007257279)
XLA Ops:
  0.7 0.7 fusion.157
  1.4 1.4 %fusion.110 = s32[]{:T(128)} fusion(s32[1,8]{1,0:T(1,128)} %param.7, s32[1,8]{1,0:T(1,128)} %param.6, s32[]{:T(128)S(6)} %axis_index.12), kind=kLoop, calls=%fused_computation.152 | loop fusion | flops 47 | bytes 72 | tf_op jit(solution)/shard_map/reduce_sum | solution.py:74
  2.8 1.4 %broadcast_multiply_fusion.2 = (f32[1024]{0:T(1024)S(1)}, f32[1024]{0:T(1024)S(1)}) fusion(f32[1024]{0:T(1024)} %bitcast.92, s32[]{:T(128)} %fusion.110), kind=kLoop, calls=%fused_computation.150 | loop fusion | flops 3072 | bytes 12292 | tf_op jit(solution)/shard_map/mul | solution.py:90
  4.2 1.8 %fusion.7 = f32[128,128]{1,0:T(8,128)S(1)} fusion(f32[1024]{0:T(1024)S(1)} %get-tuple-element.6, s32[1024]{0:T(1024)S(1)} %bitcast.67, s32[1024]{0:T(1024)S(1)} %bitcast.82, s32[128]{0:T(128)S(1)} %get-tuple-element.30, s32[1024]{0:T(1024)S(1)} %bitcast.77, s32[128]{0:T(128)S(1)} %get-tuple-element.31, s32[1024]{0:T(1024)S(1)} %bitcast.72), kind=kOutput, calls=%fused_computation.17 | convolution fusion | flops 202899456 | bytes 87040 | tf_op jit(solution)/shard_map/dot_general | solution.py:90
  6.0 1.9 %collective-permute-start.1 = (f32[32,128]{1,0:T(8,128)S(1)}, f32[32,128]{1,0:T(8,128)S(1)}, u32[]{:S(2)}, u32[]{:S(2)}) collective-permute-start(f32[32,128]{1,0:T(8,128)S(1)} %get-tuple-element.19), channel_id=1, source_target_pairs={{8,0},{16,8},{24,16},{9,1},{17,9},{25,17},{10,2},{18,10},{26,18},{... | collective-permute-start | bytes 49160 | tf_op jit(solution)/shard_map/ppermute | solution.py:31
  7.9 2.4 %collective-permute-start = (f32[32,128]{1,0:T(8,128)S(1)}, f32[32,128]{1,0:T(8,128)S(1)}, u32[]{:S(2)}, u32[]{:S(2)}) collective-permute-start(f32[32,128]{1,0:T(8,128)S(1)} %get-tuple-element.18), channel_id=1, source_target_pairs={{0,8},{8,16},{16,24},{1,9},{9,17},{17,25},{2,10},{10,18},{18,26},{... | collective-permute-start | bytes 49160 | tf_op jit(solution)/shard_map/ppermute | solution.py:28
  10.5 4.4 %fusion.2 = f32[1,1024]{1,0:T(1,128)S(1)} fusion(f32[1024,1]{0,1:T(1,128)S(1)} %bitcast.87, f32[1024]{0:T(1024)S(1)} %convert_element_type.66, f32[1024]{0:T(1024)S(1)} %convert_element_type.65, f32[1024]{0:T(1024)S(1)} %get-tuple-element.28, f32[1024]{0:T(1024)S(1)} %convert_element_type.63, f32[1024]{0:T(1024)S(1)} %convert_element_type.62, ...), kind=kOutput, calls=%fused_computation.12 | convolution fusion | flops 26214400 | bytes 32768 | tf_op jit(solution)/shard_map/dot_general | solution.py:89
  15.1 2.4 %collective-permute-start.3 = (f32[192,32]{1,0:T(8,128)S(1)}, f32[192,32]{1,0:T(8,128)S(1)}, u32[]{:S(2)}, u32[]{:S(2)}) collective-permute-start(f32[192,32]{1,0:T(8,128)S(1)} %get-tuple-element.13), channel_id=1, source_target_pairs={{1,0},{2,1},{3,2},{4,3},{5,4},{6,5},{7,6},{9,8},{10,9},{11,10},{12... | collective-permute-start | bytes 73736 | tf_op jit(solution)/shard_map/ppermute | solution.py:31
  17.5 4.3 %collective-permute-start.2 = (f32[192,32]{1,0:T(8,128)S(1)}, f32[192,32]{1,0:T(8,128)S(1)}, u32[]{:S(2)}, u32[]{:S(2)}) collective-permute-start(f32[192,32]{1,0:T(8,128)S(1)} %get-tuple-element.12), channel_id=1, source_target_pairs={{0,1},{1,2},{2,3},{3,4},{4,5},{5,6},{6,7},{8,9},{9,10},{10,11},{11... | collective-permute-start | bytes 73736 | tf_op jit(solution)/shard_map/ppermute | solution.py:28
  22.1 6.2 %gather_fusion = f32[1024]{0:T(1024)S(1)} fusion(f32[262144]{0:T(1024)S(1)} %bitcast.65, s32[1024]{0:T(1024)S(1)} %broadcast_clamp_fusion.1), kind=kCustom, calls=%fused_computation | custom fusion | bytes 12288 | tf_op jit(solution)/shard_map/gather | solution.py:80
  28.3 0.4 fusion.39
  29.1 6.2 %gather_fusion.1 = f32[1024]{0:T(1024)S(1)} fusion(f32[16384]{0:T(1024)S(1)} %convolution_bitcast_fusion.2, s32[1024]{0:T(1024)S(1)} %broadcast_clamp_fusion), kind=kCustom, calls=%fused_computation.1 | custom fusion | bytes 12288 | tf_op jit(solution)/shard_map/gather | solution.py:94
  35.3 0.7 broadcast_multiply_fusion.1
  36.0 1.8 %fusion.5 = f32[128,128]{1,0:T(8,128)S(1)} fusion(f32[1024]{0:T(1024)S(1)} %get-tuple-element.4, s32[1024]{0:T(1024)S(1)} %bitcast.70, s32[1024]{0:T(1024)S(1)} %bitcast.85, s32[128]{0:T(128)S(1)} %get-tuple-element.30, s32[1024]{0:T(1024)S(1)} %bitcast.80, s32[128]{0:T(128)S(1)} %get-tuple-element.31, s32[1024]{0:T(1024)S(1)} %bitcast.75), kind=kOutput, calls=%fused_computation.15 | convolution fusion | flops 202899456 | bytes 87040 | tf_op jit(solution)/shard_map/dot_general | solution.py:90
  37.8 2.6 %collective-permute-start.5 = (f32[32,128]{1,0:T(8,128)S(1)}, f32[32,128]{1,0:T(8,128)S(1)}, u32[]{:S(2)}, u32[]{:S(2)}) collective-permute-start(f32[32,128]{1,0:T(8,128)S(1)} %get-tuple-element.17), channel_id=1, source_target_pairs={{8,0},{16,8},{24,16},{9,1},{17,9},{25,17},{10,2},{18,10},{26,18},{... | collective-permute-start | bytes 49160 | tf_op jit(solution)/shard_map/ppermute | solution.py:31
  40.4 1.9 %collective-permute-start.4 = (f32[32,128]{1,0:T(8,128)S(1)}, f32[32,128]{1,0:T(8,128)S(1)}, u32[]{:S(2)}, u32[]{:S(2)}) collective-permute-start(f32[32,128]{1,0:T(8,128)S(1)} %get-tuple-element.16), channel_id=1, source_target_pairs={{0,8},{8,16},{16,24},{1,9},{9,17},{17,25},{2,10},{10,18},{18,26},{... | collective-permute-start | bytes 49160 | tf_op jit(solution)/shard_map/ppermute | solution.py:28
  42.3 3.1 %collective-permute-done.4 = f32[32,128]{1,0:T(8,128)S(1)} collective-permute-done((f32[32,128]{1,0:T(8,128)S(1)}, f32[32,128]{1,0:T(8,128)S(1)}, u32[]{:S(2)}, u32[]{:S(2)}) %collective-permute-start.4) | collective-permute-done | bytes 16416 | tf_op jit(solution)/shard_map/ppermute | solution.py:28
  45.5 1.9 %collective-permute-start.7 = (f32[192,32]{1,0:T(8,128)S(1)}, f32[192,32]{1,0:T(8,128)S(1)}, u32[]{:S(2)}, u32[]{:S(2)}) collective-permute-start(f32[192,32]{1,0:T(8,128)S(1)} %get-tuple-element.11), channel_id=1, source_target_pairs={{1,0},{2,1},{3,2},{4,3},{5,4},{6,5},{7,6},{9,8},{10,9},{11,10},{12... | collective-permute-start | bytes 73736 | tf_op jit(solution)/shard_map/ppermute | solution.py:31
  47.5 5.0 %collective-permute-start.6 = (f32[192,32]{1,0:T(8,128)S(1)}, f32[192,32]{1,0:T(8,128)S(1)}, u32[]{:S(2)}, u32[]{:S(2)}) collective-permute-start(f32[192,32]{1,0:T(8,128)S(1)} %get-tuple-element.10), channel_id=1, source_target_pairs={{0,1},{1,2},{2,3},{3,4},{4,5},{5,6},{6,7},{8,9},{9,10},{10,11},{11... | collective-permute-start | bytes 73736 | tf_op jit(solution)/shard_map/ppermute | solution.py:28
  52.5 4.4 %fusion.1 = f32[1,1024]{1,0:T(1,128)S(1)} fusion(f32[1024,1]{0,1:T(1,128)S(1)} %bitcast.89, f32[1024]{0:T(1024)S(1)} %convert_element_type.66, f32[1024]{0:T(1024)S(1)} %convert_element_type.65, f32[1024]{0:T(1024)S(1)} %get-tuple-element.28, f32[1024]{0:T(1024)S(1)} %convert_element_type.63, f32[1024]{0:T(1024)S(1)} %convert_element_type.62, ...), kind=kOutput, calls=%fused_computation.11 | convolution fusion | flops 26214400 | bytes 32768 | tf_op jit(solution)/shard_map/dot_general | solution.py:89
  56.9 0.4 fusion.49
  57.8 6.2 %gather_fusion.2 = f32[1024]{0:T(1024)S(1)} fusion(f32[16384]{0:T(1024)S(1)} %convolution_bitcast_fusion.1, s32[1024]{0:T(1024)S(1)} %broadcast_clamp_fusion), kind=kCustom, calls=%fused_computation.2 | custom fusion | bytes 12288 | tf_op jit(solution)/shard_map/gather | solution.py:94
  63.9 0.7 broadcast_multiply_fusion
  64.6 1.8 %fusion.3 = f32[128,128]{1,0:T(8,128)S(1)} fusion(f32[1024]{0:T(1024)S(1)} %get-tuple-element.2, s32[1024]{0:T(1024)S(1)} %bitcast.71, s32[1024]{0:T(1024)S(1)} %bitcast.86, s32[128]{0:T(128)S(1)} %get-tuple-element.30, s32[1024]{0:T(1024)S(1)} %bitcast.81, s32[128]{0:T(128)S(1)} %get-tuple-element.31, s32[1024]{0:T(1024)S(1)} %bitcast.76), kind=kOutput, calls=%fused_computation.13 | convolution fusion | flops 202899456 | bytes 87040 | tf_op jit(solution)/shard_map/dot_general | solution.py:90
  66.4 1.9 %collective-permute-start.9 = (f32[32,128]{1,0:T(8,128)S(1)}, f32[32,128]{1,0:T(8,128)S(1)}, u32[]{:S(2)}, u32[]{:S(2)}) collective-permute-start(f32[32,128]{1,0:T(8,128)S(1)} %get-tuple-element.15), channel_id=1, source_target_pairs={{8,0},{16,8},{24,16},{9,1},{17,9},{25,17},{10,2},{18,10},{26,18},{... | collective-permute-start | bytes 49160 | tf_op jit(solution)/shard_map/ppermute | solution.py:31
  68.3 2.4 %collective-permute-start.8 = (f32[32,128]{1,0:T(8,128)S(1)}, f32[32,128]{1,0:T(8,128)S(1)}, u32[]{:S(2)}, u32[]{:S(2)}) collective-permute-start(f32[32,128]{1,0:T(8,128)S(1)} %get-tuple-element.14), channel_id=1, source_target_pairs={{0,8},{8,16},{16,24},{1,9},{9,17},{17,25},{2,10},{10,18},{18,26},{... | collective-permute-start | bytes 49160 | tf_op jit(solution)/shard_map/ppermute | solution.py:28
  70.8 2.6 %collective-permute-done.8 = f32[32,128]{1,0:T(8,128)S(1)} collective-permute-done((f32[32,128]{1,0:T(8,128)S(1)}, f32[32,128]{1,0:T(8,128)S(1)}, u32[]{:S(2)}, u32[]{:S(2)}) %collective-permute-start.8) | collective-permute-done | bytes 16416 | tf_op jit(solution)/shard_map/ppermute | solution.py:28
  73.5 1.9 %collective-permute-start.11 = (f32[192,32]{1,0:T(8,128)S(1)}, f32[192,32]{1,0:T(8,128)S(1)}, u32[]{:S(2)}, u32[]{:S(2)}) collective-permute-start(f32[192,32]{1,0:T(8,128)S(1)} %get-tuple-element.9), channel_id=1, source_target_pairs={{1,0},{2,1},{3,2},{4,3},{5,4},{6,5},{7,6},{9,8},{10,9},{11,10},{12... | collective-permute-start | bytes 73736 | tf_op jit(solution)/shard_map/ppermute | solution.py:31
  75.4 5.0 %collective-permute-start.10 = (f32[192,32]{1,0:T(8,128)S(1)}, f32[192,32]{1,0:T(8,128)S(1)}, u32[]{:S(2)}, u32[]{:S(2)}) collective-permute-start(f32[192,32]{1,0:T(8,128)S(1)} %get-tuple-element.8), channel_id=1, source_target_pairs={{0,1},{1,2},{2,3},{3,4},{4,5},{5,6},{6,7},{8,9},{9,10},{10,11},{11... | collective-permute-start | bytes 73736 | tf_op jit(solution)/shard_map/ppermute | solution.py:28
  80.5 4.4 %fusion = f32[1,1024]{1,0:T(1,128)S(1)} fusion(f32[1024,1]{0,1:T(1,128)S(1)} %bitcast.88, f32[1024]{0:T(1024)S(1)} %convert_element_type.66, f32[1024]{0:T(1024)S(1)} %convert_element_type.65, f32[1024]{0:T(1024)S(1)} %get-tuple-element.28, f32[1024]{0:T(1024)S(1)} %convert_element_type.63, f32[1024]{0:T(1024)S(1)} %convert_element_type.62, ...), kind=kOutput, calls=%fused_computation.10 | convolution fusion | flops 26214400 | bytes 32768 | tf_op jit(solution)/shard_map/dot_general | solution.py:89
  85.7 6.2 %gather_fusion.3 = f32[1024]{0:T(1024)S(1)} fusion(f32[16384]{0:T(1024)S(1)} %convolution_bitcast_fusion, s32[1024]{0:T(1024)S(1)} %broadcast_clamp_fusion), kind=kCustom, calls=%fused_computation.3 | custom fusion | bytes 12288 | tf_op jit(solution)/shard_map/gather | solution.py:94
  91.9 1.3 %fusion.108 = (f32[1024]{0:T(1024)}, f32[1024]{0:T(1024)}) fusion(s32[]{:T(128)} %fusion.110, f32[1024]{0:T(1024)S(1)} %gather_fusion, f32[1024]{0:T(1024)S(1)} %bitcast.94, f32[1024]{0:T(1024)S(1)} %gather_fusion.3, f32[1024]{0:T(1024)S(1)} %get-tuple-element.3), kind=kLoop, calls=%fused_computation.144 | loop fusion | flops 9216 | bytes 24580 | tf_op jit(solution)/shard_map/jit(_where)/select_n | solution.py:99
  (38 shorter events, 2.3 us)
Async XLA Ops:
  0.6 9.7 %copy-start.1 = (s32[4,1,1024]{2,1,0:T(1,128)S(1)}, s32[4,1,1024]{2,1,0:T(1,128)}, u32[]{:S(2)}) copy-start(s32[4,1,1024]{2,1,0:T(1,128)} %param.5) | copy-start | bytes 49156
  6.0 9.0 %collective-permute-start.1 = (f32[32,128]{1,0:T(8,128)S(1)}, f32[32,128]{1,0:T(8,128)S(1)}, u32[]{:S(2)}, u32[]{:S(2)}) collective-permute-start(f32[32,128]{1,0:T(8,128)S(1)} %get-tuple-element.19), channel_id=1, source_target_pairs={{8,0},{16,8},{24,16},{9,1},{17,9},{25,17},{10,2},{18,10},{26,18},{... | collective-permute-start | bytes 49160 | tf_op jit(solution)/shard_map/ppermute | solution.py:31
  7.9 7.1 %collective-permute-start = (f32[32,128]{1,0:T(8,128)S(1)}, f32[32,128]{1,0:T(8,128)S(1)}, u32[]{:S(2)}, u32[]{:S(2)}) collective-permute-start(f32[32,128]{1,0:T(8,128)S(1)} %get-tuple-element.18), channel_id=1, source_target_pairs={{0,8},{8,16},{16,24},{1,9},{9,17},{17,25},{2,10},{10,18},{18,26},{... | collective-permute-start | bytes 49160 | tf_op jit(solution)/shard_map/ppermute | solution.py:28
  10.5 11.4 %copy-start = (f32[512,512]{1,0:T(8,128)S(1)}, f32[512,512]{1,0:T(8,128)}, u32[]{:S(2)}) copy-start(f32[512,512]{1,0:T(8,128)} %param.9) | copy-start | bytes 3145732
  15.1 13.2 %collective-permute-start.3 = (f32[192,32]{1,0:T(8,128)S(1)}, f32[192,32]{1,0:T(8,128)S(1)}, u32[]{:S(2)}, u32[]{:S(2)}) collective-permute-start(f32[192,32]{1,0:T(8,128)S(1)} %get-tuple-element.13), channel_id=1, source_target_pairs={{1,0},{2,1},{3,2},{4,3},{5,4},{6,5},{7,6},{9,8},{10,9},{11,10},{12... | collective-permute-start | bytes 73736 | tf_op jit(solution)/shard_map/ppermute | solution.py:31
  17.5 10.8 %collective-permute-start.2 = (f32[192,32]{1,0:T(8,128)S(1)}, f32[192,32]{1,0:T(8,128)S(1)}, u32[]{:S(2)}, u32[]{:S(2)}) collective-permute-start(f32[192,32]{1,0:T(8,128)S(1)} %get-tuple-element.12), channel_id=1, source_target_pairs={{0,1},{1,2},{2,3},{3,4},{4,5},{5,6},{6,7},{8,9},{9,10},{10,11},{11... | collective-permute-start | bytes 73736 | tf_op jit(solution)/shard_map/ppermute | solution.py:28
  37.8 4.5 %collective-permute-start.5 = (f32[32,128]{1,0:T(8,128)S(1)}, f32[32,128]{1,0:T(8,128)S(1)}, u32[]{:S(2)}, u32[]{:S(2)}) collective-permute-start(f32[32,128]{1,0:T(8,128)S(1)} %get-tuple-element.17), channel_id=1, source_target_pairs={{8,0},{16,8},{24,16},{9,1},{17,9},{25,17},{10,2},{18,10},{26,18},{... | collective-permute-start | bytes 49160 | tf_op jit(solution)/shard_map/ppermute | solution.py:31
  40.4 5.1 %collective-permute-start.4 = (f32[32,128]{1,0:T(8,128)S(1)}, f32[32,128]{1,0:T(8,128)S(1)}, u32[]{:S(2)}, u32[]{:S(2)}) collective-permute-start(f32[32,128]{1,0:T(8,128)S(1)} %get-tuple-element.16), channel_id=1, source_target_pairs={{0,8},{8,16},{16,24},{1,9},{9,17},{17,25},{2,10},{10,18},{18,26},{... | collective-permute-start | bytes 49160 | tf_op jit(solution)/shard_map/ppermute | solution.py:28
  45.5 11.4 %collective-permute-start.7 = (f32[192,32]{1,0:T(8,128)S(1)}, f32[192,32]{1,0:T(8,128)S(1)}, u32[]{:S(2)}, u32[]{:S(2)}) collective-permute-start(f32[192,32]{1,0:T(8,128)S(1)} %get-tuple-element.11), channel_id=1, source_target_pairs={{1,0},{2,1},{3,2},{4,3},{5,4},{6,5},{7,6},{9,8},{10,9},{11,10},{12... | collective-permute-start | bytes 73736 | tf_op jit(solution)/shard_map/ppermute | solution.py:31
  47.5 9.5 %collective-permute-start.6 = (f32[192,32]{1,0:T(8,128)S(1)}, f32[192,32]{1,0:T(8,128)S(1)}, u32[]{:S(2)}, u32[]{:S(2)}) collective-permute-start(f32[192,32]{1,0:T(8,128)S(1)} %get-tuple-element.10), channel_id=1, source_target_pairs={{0,1},{1,2},{2,3},{3,4},{4,5},{5,6},{6,7},{8,9},{9,10},{10,11},{11... | collective-permute-start | bytes 73736 | tf_op jit(solution)/shard_map/ppermute | solution.py:28
  66.4 4.3 %collective-permute-start.9 = (f32[32,128]{1,0:T(8,128)S(1)}, f32[32,128]{1,0:T(8,128)S(1)}, u32[]{:S(2)}, u32[]{:S(2)}) collective-permute-start(f32[32,128]{1,0:T(8,128)S(1)} %get-tuple-element.15), channel_id=1, source_target_pairs={{8,0},{16,8},{24,16},{9,1},{17,9},{25,17},{10,2},{18,10},{26,18},{... | collective-permute-start | bytes 49160 | tf_op jit(solution)/shard_map/ppermute | solution.py:31
  68.3 5.1 %collective-permute-start.8 = (f32[32,128]{1,0:T(8,128)S(1)}, f32[32,128]{1,0:T(8,128)S(1)}, u32[]{:S(2)}, u32[]{:S(2)}) collective-permute-start(f32[32,128]{1,0:T(8,128)S(1)} %get-tuple-element.14), channel_id=1, source_target_pairs={{0,8},{8,16},{16,24},{1,9},{9,17},{17,25},{2,10},{10,18},{18,26},{... | collective-permute-start | bytes 49160 | tf_op jit(solution)/shard_map/ppermute | solution.py:28
  73.5 11.4 %collective-permute-start.11 = (f32[192,32]{1,0:T(8,128)S(1)}, f32[192,32]{1,0:T(8,128)S(1)}, u32[]{:S(2)}, u32[]{:S(2)}) collective-permute-start(f32[192,32]{1,0:T(8,128)S(1)} %get-tuple-element.9), channel_id=1, source_target_pairs={{1,0},{2,1},{3,2},{4,3},{5,4},{6,5},{7,6},{9,8},{10,9},{11,10},{12... | collective-permute-start | bytes 73736 | tf_op jit(solution)/shard_map/ppermute | solution.py:31
  75.4 9.5 %collective-permute-start.10 = (f32[192,32]{1,0:T(8,128)S(1)}, f32[192,32]{1,0:T(8,128)S(1)}, u32[]{:S(2)}, u32[]{:S(2)}) collective-permute-start(f32[192,32]{1,0:T(8,128)S(1)} %get-tuple-element.8), channel_id=1, source_target_pairs={{0,1},{1,2},{2,3},{3,4},{4,5},{5,6},{6,7},{8,9},{9,10},{10,11},{11... | collective-permute-start | bytes 73736 | tf_op jit(solution)/shard_map/ppermute | solution.py:28
where the time goes:
time: 93.7 us; the launch traced here: 93.2 us
  starting transfers between devices  33.8 us (36%)
  local copies, waits for them, and re-layouts  25.9 us (28%)
  matrix products  21 us (22%)
  waiting for transfers between devices  5.8 us (6%)
  other arithmetic  5.62 us (6%)
  between operations  1.05 us (1%)
    ppermute x6, starting transfers between devices, with_halo(): lax.ppermute(lax.slice_in_dim(block, block.shape[dim] - width, None, axis...  21.1 us
    gather x3, local copies, waits for them, and re-layouts, body(): sampled = background.reshape(-1)[cell_ids]  18.5 us
    dot_general x3, matrix products, body(): forward = jnp.dot(shot_dose, kernel, precision=EXACT_MODE)  13.3 us
    ppermute x6, starting transfers between devices, with_halo(): lax.ppermute(lax.slice_in_dim(block, 0, width, axis=dim), axis, backward)  12.7 us
    gather x1, local copies, waits for them, and re-layouts, body(): sensitive = pixel_gain.reshape(-1)[pixel_ids]  6.15 us
    ppermute x6, waiting for transfers between devices, with_halo(): lax.ppermute(lax.slice_in_dim(block, block.shape[dim] - width, None, axis...  5.78 us
    dot_general x3, matrix products, body(): jnp.dot(downward.T, shot_dose[:, None] * across, precision=EXACT_MODE)  5.3 us
    mul x3, other arithmetic, body(): shot_dose[:, None] * across  2.78 us
  transfers between devices with their start and end apart: 12, of which 2 were waited for; matrix products, arithmetic and copies ran while one was open for 21% of the time, Pallas kernels for 0%

commit v1 on v0

v1 whole, which is shorter than its diff:
```python
import functools
import math

import jax
import jax.numpy as jnp
from jax import lax
from jax.experimental import pallas as pl
from jax.experimental.pallas import tpu as pltpu
from jax.sharding import PartitionSpec as P

BLK = 128
ITERS = 3
CELL = 4
BETA = 16
REACH = 32
LANES = 128

FORWARD_RANGE = 4.0
BACK_RATIO = 0.75
TARGET_LEVEL = 1.0
MESH = pl.DeviceIdType.MESH
NEAR = [(-1, 0), (1, 0), (0, -1), (0, 1), (-1, -1), (-1, 1), (1, -1), (1, 1)]


def halves(value):
    high = value.astype(jnp.bfloat16)
    low = (value - high.astype(jnp.float32)).astype(jnp.bfloat16)
    return high, low


def mxu(a, b):
    return jnp.dot(a, b, preferred_element_type=jnp.float32)


def spread(distance):
    scaled = distance.astype(jnp.float32) / BETA
    inside = jnp.abs(distance) <= REACH
    return jnp.where(inside, jnp.exp(-scaled * scaled) / (math.sqrt(math.pi) * BETA), 0.0)


def covered(low, high, cell):
    edge = cell.astype(jnp.float32) * CELL
    part = jnp.minimum(high, edge + CELL) - jnp.maximum(low, edge)
    return jnp.maximum(part, 0.0) * (1.0 / CELL)


def kernel(
    rows, cols,
    boxes, counts, tails, doses, gain_hbm, dose_out, exposure_out,
    gain, gain2, pairs, column, dose_column, down_t, side_t, across, downward,
    wx2, wy2, wy_own, wy_halo, wx_halo, sens,
    coarse, coarse_t, corner_out, halo_y, halo_x, corner_in,
    gain_sem, send_sem, recv_sem,
):
    slots = doses.shape[1]
    tile = gain.shape[0]
    cg = tile // CELL
    r, c = lax.axis_index("row"), lax.axis_index("col")
    halo_y[...] = jnp.zeros_like(halo_y)
    halo_x[...] = jnp.zeros_like(halo_x)
    corner_in[...] = jnp.zeros_like(corner_in)

    def present(dr, dc):
        tests = []
        if dr:
            tests.append(r > 0 if dr < 0 else r < rows - 1)
        if dc:
            tests.append(c > 0 if dc < 0 else c < cols - 1)
        return functools.reduce(jnp.logical_and, tests)

    barrier = pltpu.get_barrier_semaphore()
    for dr, dc in NEAR:
        @pl.when(present(dr, dc))
        def _():
            pl.semaphore_signal(barrier, inc=1, device_id=(r + dr, c + dc), device_id_type=MESH)

    fetch = pltpu.make_async_copy(gain_hbm, gain, gain_sem)
    fetch.start()

    x0, y0, x1, y1 = (boxes[k].astype(jnp.float32) for k in range(4))
    peers = lax.broadcasted_iota(jnp.int32, counts.shape, 1)
    totals = (counts[...] - 1) * BLK + tails[...]
    total = jnp.sum(jnp.where(peers == c, totals, 0), axis=1, keepdims=True)
    live = lax.broadcasted_iota(jnp.int32, (1, slots), 1) < total
    dose = jnp.where(live, doses[...], 0.0)

    stack = jnp.concatenate([x0, x1, y0, y1, dose, dose, dose, dose], axis=0)
    column[...] = jnp.transpose(stack)
    cell_row = lax.broadcasted_iota(jnp.int32, (slots, cg), 1)
    downward[...] = covered(column[:, 2:3], column[:, 3:4], cell_row).astype(jnp.bfloat16)
    side = lax.broadcasted_iota(jnp.int32, (2 * REACH, slots), 0)
    side = jnp.where(side < REACH, side, side + (cg - 2 * REACH))
    side_t[...] = covered(x0, x1, side)
    across[...] = covered(column[:, 0:1], column[:, 1:2], cell_row).astype(jnp.bfloat16)
    down_t[...] = covered(y0, y1, lax.broadcasted_iota(jnp.int32, (cg, slots), 0))
    lane = lax.broadcasted_iota(jnp.int32, (8, LANES), 1)

    def copies(k):
        made = []
        for n, (dr, dc) in enumerate(NEAR):
            ys, xs = (0 if dr < 0 else 1), (0 if dc < 0 else 1)
            if dc == 0:
                src = coarse.at[k, pl.ds(ys * (cg - REACH), REACH), :]
                dst = halo_y.at[k, pl.ds((1 - ys) * REACH, REACH), :]
            elif dr == 0:
                src = coarse_t.at[k, pl.ds(xs * REACH, REACH), :]
                dst = halo_x.at[k, pl.ds((1 - xs) * REACH, REACH), :]
            else:
                src = corner_out.at[k, 2 * xs + ys]
                dst = corner_in.at[k, 2 * (1 - xs) + (1 - ys)]
            made.append(pltpu.make_async_remote_copy(
                src_ref=src, dst_ref=dst,
                send_sem=send_sem.at[k, n], recv_sem=recv_sem.at[k, n],
                device_id=(r + dr, c + dc), device_id_type=MESH,
            ))
        return made

    def send(k, dose, first):
        high, low = halves(side_t[...] * dose)
        both = mxu(jnp.concatenate([high, low], axis=0), downward[...])
        edges = both[:2 * REACH] + both[2 * REACH:]
        coarse_t[k] = edges
        for xs in range(2):
            for ys in range(2):
                packed = jnp.zeros((8, LANES), jnp.float32)
                for q in range(REACH // 8):
                    part = edges[xs * REACH + 8 * q:xs * REACH + 8 * q + 8]
                    shift = (REACH * q - ys * (cg - REACH)) % LANES
                    if shift:
                        part = pltpu.roll(part, shift, 1)
                    packed = jnp.where(lane // REACH == q, part, packed)
                corner_out[k, 2 * xs + ys] = packed
        made = copies(k)
        if first:
            up = (r > 0).astype(jnp.int32) + (r < rows - 1).astype(jnp.int32) + 1
            across_count = (c > 0).astype(jnp.int32) + (c < cols - 1).astype(jnp.int32) + 1
            pl.semaphore_wait(barrier, up * across_count - 1)
        for n in range(2, 8):
            @pl.when(present(*NEAR[n]))
            def _():
                made[n].start()
        high, low = halves(down_t[...] * dose)
        both = mxu(jnp.concatenate([high, low], axis=0), across[...])
        coarse[k] = both[:cg] + both[cg:]
        for n in range(2):
            @pl.when(present(*NEAR[n]))
            def _():
                made[n].start()
        return made

    def weighted(value, weights2, weights):
        high, low = halves(value)
        lhs = jnp.concatenate(
            [jnp.concatenate([high, high], axis=1), jnp.concatenate([low, low], axis=1)], axis=0
        )
        both = mxu(lhs, weights2[...])
        count = value.shape[0]
        return jnp.sum((both[:count] + both[count:]) * weights[...], axis=0, keepdims=True)

    made = send(0, dose, True)

    two_x, two_y = boxes[0] + boxes[2], boxes[1] + boxes[3]
    cell_x, cell_y = two_x >> 3, two_y >> 3
    own = lax.broadcasted_iota(jnp.int32, (cg, slots), 0)
    around = lax.broadcasted_iota(jnp.int32, (2 * REACH, slots), 0)
    around = jnp.where(around < REACH, around - REACH, around + (cg - REACH))
    high, low = halves(spread(own - cell_x))
    wx2[0:cg, :] = high
    wx2[cg:2 * cg, :] = low
    weight = spread(own - cell_y)
    wy_own[...] = weight
    high, low = halves(weight)
    wy2[0:cg, :] = high
    wy2[2 * cg:3 * cg, :] = low
    weight = spread(around - cell_y)
    wy_halo[...] = weight
    high, low = halves(weight)
    blank = jnp.zeros((cg - 2 * REACH, slots), jnp.bfloat16)
    wy2[cg:2 * cg, :] = jnp.concatenate([high, blank], axis=0)
    wy2[3 * cg:4 * cg, :] = jnp.concatenate([low, blank], axis=0)
    wx_halo[...] = spread(around - cell_x)

    table = 0.5 * lax.erf((lane - LANES // 2).astype(jnp.float32) * (0.5 / FORWARD_RANGE))

    def look(index):
        index = jnp.clip(index, 0, LANES - 1)
        return jnp.take_along_axis(table, index, axis=1, mode="promise_in_bounds")

    blocks = slots // LANES
    half = LANES // 2

    def build(g, totals):
        start = pl.multiple_of(g * 8, 8)
        group = column[pl.ds(start, 8), :]
        wide = [
            jnp.broadcast_to(group[:, m:m + 1], (8, LANES)) for m in range(5)
        ]
        bx0, bx1, by0, by1 = (w.astype(jnp.int32) * 2 - half for w in wide[:4])
        fresh = []
        for b in range(blocks):
            at = slice(b * LANES, (b + 1) * LANES)
            px = jnp.broadcast_to(two_x[:, at], (8, LANES))
            py = jnp.broadcast_to(two_y[:, at], (8, LANES))
            gx = look(px - bx0) - look(px - bx1)
            gy = look(py - by0) - look(py - by1)
            value = gx * gy
            pairs[pl.ds(start, 8), at] = value
            fresh.append(totals[b] + value * wide[4])
        return tuple(fresh)

    zero = tuple(jnp.zeros((8, LANES), jnp.float32) for _ in range(blocks))
    sums = lax.fori_loop(0, slots // 8, build, zero)
    forward = jnp.concatenate([jnp.sum(s, axis=0, keepdims=True) for s in sums], axis=1)

    fetch.wait()
    high, low = halves(gain[...])
    gain2[:, 0:tile] = high
    gain2[:, tile:2 * tile] = low
    step = 256

    def sample(i, _):
        at = pl.ds(pl.multiple_of(i * step, step), step)
        mid_x = (boxes[0, :, at] + boxes[2, :, at]) >> 1
        mid_y = (boxes[1, :, at] + boxes[3, :, at]) >> 1
        pixel = lax.broadcasted_iota(jnp.int32, (tile, step), 0)
        hot = jnp.where(pixel == mid_x, 1.0, 0.0).astype(jnp.bfloat16)
        taken = mxu(gain2[...], jnp.concatenate([hot, hot], axis=0))
        sens[:, at] = jnp.sum(jnp.where(pixel == mid_y, taken, 0.0), axis=0, keepdims=True)
        return 0

    lax.fori_loop(0, slots // step, sample, 0)

    for k in range(ITERS):
        if k:
            made = send(k, dose, False)
            dose_column[...] = jnp.transpose(jnp.broadcast_to(dose, (8, slots)))

            def add(g, totals):
                start = pl.multiple_of(g * 8, 8)
                wide = jnp.broadcast_to(dose_column[pl.ds(start, 8), 0:1], (8, LANES))
                return tuple(
                    totals[b] + pairs[pl.ds(start, 8), b * LANES:(b + 1) * LANES] * wide
                    for b in range(blocks)
                )

            sums = lax.fori_loop(0, slots // 8, add, zero, unroll=4)
            forward = jnp.concatenate([jnp.sum(s, axis=0, keepdims=True) for s in sums], axis=1)
        background = weighted(coarse[k], wx2, wy_own)
        for n, (dr, dc) in enumerate(NEAR):
            @pl.when(present(-dr, -dc))
            def _():
                made[n].wait_recv()
        background += weighted(halo_y[k], wx2, wy_halo)
        strips = []
        for xs in range(2):
            for q in range(REACH // 8):
                top, low_part = corner_in[k, 2 * xs], corner_in[k, 2 * xs + 1]
                shift = (-REACH * q) % LANES
                if shift:
                    top = pltpu.roll(top, shift, 1)
                shift = (REACH - REACH * q) % LANES
                if shift:
                    low_part = pltpu.roll(low_part, shift, 1)
                strips.append(jnp.where(
                    lane < REACH, top, jnp.where(lane < 2 * REACH, low_part, 0.0)
                ))
        sides = jnp.concatenate([halo_x[k], jnp.concatenate(strips, axis=0)], axis=1)
        background += weighted(sides, wy2, wx_halo)
        exposure = sens[...] * (forward + BACK_RATIO * background) * (1.0 / (1.0 + BACK_RATIO))
        dose = jnp.where(live, dose * TARGET_LEVEL / jnp.where(live, exposure, 1.0), 0.0)
    dose_out[...] = dose
    exposure_out[...] = jnp.where(live, exposure, 0.0)
    for k in range(ITERS):
        made = copies(k)
        for n in range(8):
            @pl.when(present(*NEAR[n]))
            def _():
                made[n].wait_send()


def body(rows, cols, shot_boxes, block_counts, tail_shots, doses, pixel_gain):
    slots = doses.shape[1]
    tile = pixel_gain.shape[0]
    cg = tile // CELL
    f32, bf16 = jnp.float32, jnp.bfloat16
    vmem = pl.BlockSpec(memory_space=pltpu.VMEM)
    return pl.pallas_call(
        functools.partial(kernel, rows, cols),
        out_shape=(jax.ShapeDtypeStruct((1, slots), f32),) * 2,
        in_specs=[vmem] * 4 + [pl.BlockSpec(memory_space=pl.ANY)],
        out_specs=(vmem, vmem),
        scratch_shapes=[
            pltpu.VMEM((tile, tile), f32),
            pltpu.VMEM((tile, 2 * tile), bf16),
            pltpu.VMEM((slots, slots), f32),
            pltpu.VMEM((slots, 8), f32),
            pltpu.VMEM((slots, 8), f32),
            pltpu.VMEM((cg, slots), f32),
            pltpu.VMEM((2 * REACH, slots), f32),
            pltpu.VMEM((slots, cg), bf16),
            pltpu.VMEM((slots, cg), bf16),
            pltpu.VMEM((2 * cg, slots), bf16),
            pltpu.VMEM((4 * cg, slots), bf16),
            pltpu.VMEM((cg, slots), f32),
            pltpu.VMEM((2 * REACH, slots), f32),
            pltpu.VMEM((2 * REACH, slots), f32),
            pltpu.VMEM((1, slots), f32),
            pltpu.VMEM((ITERS, cg, cg), f32),
            pltpu.VMEM((ITERS, 2 * REACH, cg), f32),
            pltpu.VMEM((ITERS, 4, 8, LANES), f32),
            pltpu.VMEM((ITERS, 2 * REACH, cg), f32),
            pltpu.VMEM((ITERS, 2 * REACH, cg), f32),
            pltpu.VMEM((ITERS, 4, 8, LANES), f32),
            pltpu.SemaphoreType.DMA,
            pltpu.SemaphoreType.DMA((ITERS, 8)),
            pltpu.SemaphoreType.DMA((ITERS, 8)),
        ],
        compiler_params=pltpu.CompilerParams(
            collective_id=0, has_side_effects=True, vmem_limit_bytes=40 * 1024 * 1024
        ),
    )(shot_boxes, block_counts, tail_shots, doses, pixel_gain)


def solution(mesh):
    placed = (
        P(None, "row", "col"),
        P("row", None),
        P("row", None),
        P("row", "col"),
        P("row", "col"),
    )
    return jax.shard_map(
        functools.partial(body, mesh.shape["row"], mesh.shape["col"]),
        mesh=mesh,
        in_specs=placed,
        out_specs=(P("row", "col"), P("row", "col")),
        check_vma=False,
    )
```

time: 93.7 us -> 52.8 us (0.56)
  the two profiles are of different devices: /device:TPU:6 before, /device:TPU:1 now
where the time goes in v1:
time: 52.8 us; the launch traced here: 52.6 us
  Pallas kernels  46.8 us (89%)
  local copies, waits for them, and re-layouts  5.12 us (10%)
  between operations  0.65 us (1%)
    pallas_call x1, Pallas kernels, body(): pl.pallas_call(functools.partial(kernel, rows, cols), out_shape=(jax.Shap...  46.8 us
    unnamed x12, local copies, waits for them, and re-layouts  5.12 us

profile of v1, /device:TPU:1, one launch (start us, length us, event | category | flops | bytes accessed | tf_op | source)
XLA Modules:
  0.0 52.6 jit_solution(3465788459269327005)
XLA Ops:
  0.6 0.0 copy-start
  0.6 1.2 %copy-done = f32[512,512]{1,0:T(8,128)S(1)} copy-done((f32[512,512]{1,0:T(8,128)S(1)}, f32[512,512]{1,0:T(8,128)}, u32[]{:S(2)}) %copy-start) | copy-done | bytes 1048600
  1.9 0.0 copy-start.1
  1.9 0.7 %copy-done.1 = s32[4,1,1024]{2,1,0:T(1,128)S(1)} copy-done((s32[4,1,1024]{2,1,0:T(1,128)S(1)}, s32[4,1,1024]{2,1,0:T(1,128)}, u32[]{:S(2)}) %copy-start.1) | copy-done | bytes 16408
  2.6 0.0 copy-start.2
  2.6 0.7 %copy-done.2 = f32[1,1024]{1,0:T(1,128)S(1)} copy-done((f32[1,1024]{1,0:T(1,128)S(1)}, f32[1,1024]{1,0:T(1,128)}, u32[]{:S(2)}) %copy-start.2) | copy-done | bytes 4120
  3.3 0.0 copy-start.3
  3.3 0.7 %copy-done.3 = s32[1,8]{1,0:T(1,128)S(1)} copy-done((s32[1,8]{1,0:T(1,128)S(1)}, s32[1,8]{1,0:T(1,128)}, u32[]{:S(2)}) %copy-start.3) | copy-done | bytes 56
  3.9 0.0 copy-start.4
  3.9 0.7 %copy-done.4 = s32[1,8]{1,0:T(1,128)S(1)} copy-done((s32[1,8]{1,0:T(1,128)S(1)}, s32[1,8]{1,0:T(1,128)}, u32[]{:S(2)}) %copy-start.4) | copy-done | bytes 56
  4.6 46.8 %shard_map.68 = (f32[1,1024]{1,0:T(1,128)S(1)}, f32[1,1024]{1,0:T(1,128)S(1)}) custom-call(s32[4,1,1024]{2,1,0:T(1,128)S(1)} %copy-done.1, s32[1,8]{1,0:T(1,128)S(1)} %copy-done.3, s32[1,8]{1,0:T(1,128)S(1)} %copy-done.4, f32[1,1024]{1,0:T(1,128)S(1)} %copy-done.2, f32[512,512]{1,0:T(8,128)S(1)} %copy-done), custom_call_target="tpu_custom_call" | custom-call | tf_op jit(solution)/shard_map/pallas_call | solution.py:287
  51.4 0.6 %copy.9 = f32[1,1024]{1,0:T(1,128)} copy(f32[1,1024]{1,0:T(1,128)S(1)} %get-tuple-element.4) | data formatting | bytes 8192
  52.0 0.6 %copy.10 = f32[1,1024]{1,0:T(1,128)} copy(f32[1,1024]{1,0:T(1,128)S(1)} %get-tuple-element.5) | data formatting | bytes 8192
Async XLA Ops:
  0.6 1.2 %copy-start = (f32[512,512]{1,0:T(8,128)S(1)}, f32[512,512]{1,0:T(8,128)}, u32[]{:S(2)}) copy-start(f32[512,512]{1,0:T(8,128)} %gain_hbm.1) | copy-start | bytes 3145732
  1.9 0.7 %copy-start.1 = (s32[4,1,1024]{2,1,0:T(1,128)S(1)}, s32[4,1,1024]{2,1,0:T(1,128)}, u32[]{:S(2)}) copy-start(s32[4,1,1024]{2,1,0:T(1,128)} %boxes.1) | copy-start | bytes 49156
  2.6 0.7 %copy-start.2 = (f32[1,1024]{1,0:T(1,128)S(1)}, f32[1,1024]{1,0:T(1,128)}, u32[]{:S(2)}) copy-start(f32[1,1024]{1,0:T(1,128)} %doses.1) | copy-start | bytes 12292
  3.3 0.7 %copy-start.3 = (s32[1,8]{1,0:T(1,128)S(1)}, s32[1,8]{1,0:T(1,128)}, u32[]{:S(2)}) copy-start(s32[1,8]{1,0:T(1,128)} %counts.1) | copy-start | bytes 100
  3.9 0.7 %copy-start.4 = (s32[1,8]{1,0:T(1,128)S(1)}, s32[1,8]{1,0:T(1,128)}, u32[]{:S(2)}) copy-start(s32[1,8]{1,0:T(1,128)} %tails.1) | copy-start | bytes 100

commit v2 on v1

--- a/solution.py
+++ b/solution.py
@@ -14,6 +14,8 @@
 BETA = 16
 REACH = 32
 LANES = 128
+EDGE_STEP = 16
+UNROLL = 16
 
 FORWARD_RANGE = 4.0
 BACK_RATIO = 0.75
@@ -46,11 +48,12 @@
 
 def kernel(
     rows, cols,
-    boxes, counts, tails, doses, gain_hbm, dose_out, exposure_out,
-    gain, gain2, pairs, column, dose_column, down_t, side_t, across, downward,
+    box_scalar, boxes_hbm, counts_hbm, tails_hbm, doses_hbm, gain_hbm, dose_out, exposure_out,
+    boxes, counts, tails, doses, near_x, near_y, edge_x, edge_y, dose_wide,
+    gain, gain2, pairs, column, down_t, side_t, across, downward,
     wx2, wy2, wy_own, wy_halo, wx_halo, sens,
     coarse, coarse_t, corner_out, halo_y, halo_x, corner_in,
-    gain_sem, send_sem, recv_sem,
+    in_sem, send_sem, recv_sem,
 ):
     slots = doses.shape[1]
     tile = gain.shape[0]
@@ -74,8 +77,19 @@
         def _():
             pl.semaphore_signal(barrier, inc=1, device_id=(r + dr, c + dc), device_id_type=MESH)
 
-    fetch = pltpu.make_async_copy(gain_hbm, gain, gain_sem)
+    fetches = [
+        pltpu.make_async_copy(src, dst, in_sem.at[n])
+        for n, (src, dst) in enumerate((
+            (boxes_hbm, boxes), (counts_hbm, counts), (tails_hbm, tails), (doses_hbm, doses),
+            (gain_hbm, gain),
+        ))
+    ]
+    fetch = fetches[4]
+    for one in fetches[:4]:
+        one.start()
     fetch.start()
+    for one in fetches[:4]:
+        one.wait()
 
     x0, y0, x1, y1 = (boxes[k].astype(jnp.float32) for k in range(4))
     peers = lax.broadcasted_iota(jnp.int32, counts.shape, 1)
@@ -180,37 +194,59 @@
     wy2[3 * cg:4 * cg, :] = jnp.concatenate([low, blank], axis=0)
     wx_halo[...] = spread(around - cell_x)
 
-    table = 0.5 * lax.erf((lane - LANES // 2).astype(jnp.float32) * (0.5 / FORWARD_RANGE))
-
-    def look(index):
-        index = jnp.clip(index, 0, LANES - 1)
-        return jnp.take_along_axis(table, index, axis=1, mode="promise_in_bounds")
-
     blocks = slots // LANES
-    half = LANES // 2
-
-    def build(g, totals):
-        start = pl.multiple_of(g * 8, 8)
-        group = column[pl.ds(start, 8), :]
-        wide = [
-            jnp.broadcast_to(group[:, m:m + 1], (8, LANES)) for m in range(5)
-        ]
-        bx0, bx1, by0, by1 = (w.astype(jnp.int32) * 2 - half for w in wide[:4])
-        fresh = []
+    group = EDGE_STEP
+
+    def folded(row):
+        return jnp.concatenate([row[:, b * LANES:(b + 1) * LANES] for b in range(blocks)], axis=0)
+
+    def flat(square):
+        return jnp.concatenate([square[b:b + 1, :] for b in range(blocks)], axis=1)
+
+    for two, near, edges in ((folded(two_x), near_x, edge_x), (folded(two_y), near_y, edge_y)):
+        coarse_part = two // (2 * group)
+        fine = two - coarse_part * (2 * group)
+        for m in range(3):
+            for q in range(group):
+                gap = fine + ((m - 1) * 2 * group - 2 * q)
+                near[m * group + q] = 0.5 * lax.erf(gap.astype(jnp.float32) * (0.5 / FORWARD_RANGE))
+
+        def fill(p, _):
+            same, above, below = coarse_part == p, coarse_part == p + 1, coarse_part == p - 1
+            far = jnp.where(coarse_part > p, 0.5, -0.5)
+            for q in range(group):
+                value = jnp.where(above, near[2 * group + q], far)
+                value = jnp.where(below, near[q], value)
+                edges[p * group + q] = jnp.where(same, near[group + q], value)
+            return 0
+
+        lax.fori_loop(0, tile // group + 1, fill, 0)
+
+    def widen(dose):
         for b in range(blocks):
             at = slice(b * LANES, (b + 1) * LANES)
-            px = jnp.broadcast_to(two_x[:, at], (8, LANES))
-            py = jnp.broadcast_to(two_y[:, at], (8, LANES))
-            gx = look(px - bx0) - look(px - bx1)
-            gy = look(py - by0) - look(py - by1)
-            value = gx * gy
-            pairs[pl.ds(start, 8), at] = value
-            fresh.append(totals[b] + value * wide[4])
-        return tuple(fresh)
-
-    zero = tuple(jnp.zeros((8, LANES), jnp.float32) for _ in range(blocks))
-    sums = lax.fori_loop(0, slots // 8, build, zero)
-    forward = jnp.concatenate([jnp.sum(s, axis=0, keepdims=True) for s in sums], axis=1)
+            dose_wide[at, :] = jnp.transpose(jnp.broadcast_to(dose[:, at], (LANES, LANES)))
+
+    zero = tuple(jnp.zeros((blocks, LANES), jnp.float32) for _ in range(4))
+
+    def total_of(sums):
+        return flat((sums[0] + sums[1]) + (sums[2] + sums[3]))
+
+    def build(g, sums):
+        sums = list(sums)
+        kept = []
+        for n in range(UNROLL):
+            j = g * UNROLL + n
+            low_x, low_y, high_x, high_y = (box_scalar[k, 0, j] for k in range(4))
+            kept.append((edge_x[low_x] - edge_x[high_x]) * (edge_y[low_y] - edge_y[high_y]))
+        for n in range(UNROLL):
+            j = g * UNROLL + n
+            pairs[j] = kept[n]
+            sums[n % 4] += kept[n] * dose_wide[pl.ds(j, 1), :]
+        return tuple(sums)
+
+    widen(dose)
+    forward = total_of(lax.fori_loop(0, slots // UNROLL, build, zero))
 
     fetch.wait()
     high, low = halves(gain[...])
@@ -233,18 +269,16 @@
     for k in range(ITERS):
         if k:
             made = send(k, dose, False)
-            dose_column[...] = jnp.transpose(jnp.broadcast_to(dose, (8, slots)))
-
-            def add(g, totals):
-                start = pl.multiple_of(g * 8, 8)
-                wide = jnp.broadcast_to(dose_column[pl.ds(start, 8), 0:1], (8, LANES))
-                return tuple(
-                    totals[b] + pairs[pl.ds(start, 8), b * LANES:(b + 1) * LANES] * wide
-                    for b in range(blocks)
-                )
-
-            sums = lax.fori_loop(0, slots // 8, add, zero, unroll=4)
-            forward = jnp.concatenate([jnp.sum(s, axis=0, keepdims=True) for s in sums], axis=1)
+            widen(dose)
+
+            def add(g, sums):
+                sums = list(sums)
+                for n in range(16):
+                    j = g * 16 + n
+                    sums[n % 4] += pairs[j] * dose_wide[pl.ds(j, 1), :]
+                return tuple(sums)
+
+            forward = total_of(lax.fori_loop(0, slots // 16, add, zero))
         background = weighted(coarse[k], wx2, wy_own)
         for n, (dr, dc) in enumerate(NEAR):
             @pl.when(present(-dr, -dc))
@@ -287,13 +321,22 @@
     return pl.pallas_call(
         functools.partial(kernel, rows, cols),
         out_shape=(jax.ShapeDtypeStruct((1, slots), f32),) * 2,
-        in_specs=[vmem] * 4 + [pl.BlockSpec(memory_space=pl.ANY)],
+        in_specs=[pl.BlockSpec(memory_space=pltpu.SMEM)]
+        + [pl.BlockSpec(memory_space=pltpu.HBM)] * 5,
         out_specs=(vmem, vmem),
         scratch_shapes=[
+            pltpu.VMEM(shot_boxes.shape, jnp.int32),
+            pltpu.VMEM(block_counts.shape, jnp.int32),
+            pltpu.VMEM(tail_shots.shape, jnp.int32),
+            pltpu.VMEM(doses.shape, f32),
+            pltpu.VMEM((3 * EDGE_STEP, slots // LANES, LANES), f32),
+            pltpu.VMEM((3 * EDGE_STEP, slots // LANES, LANES), f32),
+            pltpu.VMEM((tile + EDGE_STEP, slots // LANES, LANES), f32),
+            pltpu.VMEM((tile + EDGE_STEP, slots // LANES, LANES), f32),
+            pltpu.VMEM((slots, LANES), f32),
             pltpu.VMEM((tile, tile), f32),
             pltpu.VMEM((tile, 2 * tile), bf16),
-            pltpu.VMEM((slots, slots), f32),
-            pltpu.VMEM((slots, 8), f32),
+            pltpu.VMEM((slots, slots // LANES, LANES), f32),
             pltpu.VMEM((slots, 8), f32),
             pltpu.VMEM((cg, slots), f32),
             pltpu.VMEM((2 * REACH, slots), f32),
@@ -311,14 +354,14 @@
             pltpu.VMEM((ITERS, 2 * REACH, cg), f32),
             pltpu.VMEM((ITERS, 2 * REACH, cg), f32),
             pltpu.VMEM((ITERS, 4, 8, LANES), f32),
-            pltpu.SemaphoreType.DMA,
+            pltpu.SemaphoreType.DMA((5,)),
             pltpu.SemaphoreType.DMA((ITERS, 8)),
             pltpu.SemaphoreType.DMA((ITERS, 8)),
         ],
         compiler_params=pltpu.CompilerParams(
-            collective_id=0, has_side_effects=True, vmem_limit_bytes=40 * 1024 * 1024
+            collective_id=0, has_side_effects=True, vmem_limit_bytes=60 * 1024 * 1024
         ),
-    )(shot_boxes, block_counts, tail_shots, doses, pixel_gain)
+    )(shot_boxes, shot_boxes, block_counts, tail_shots, doses, pixel_gain)
 
 
 def solution(mesh):

time: 52.8 us -> 28.1 us (0.53)
  Pallas kernels: 46.8 us -> 25.3 us
  local copies, waits for them, and re-layouts: 5.12 us -> 1.86 us
    pallas_call x1, Pallas kernels: 46.8 us -> 25.3 us  [body(): pl.pallas_call(functools.partial(kernel, rows, cols), out_shape=(jax.Shap...]
    unnamed x12 -> x4, local copies, waits for them, and re-layouts: 5.12 us -> 1.86 us
where the time goes in v2:
time: 28.1 us; the launch traced here: 27.8 us
  Pallas kernels  25.3 us (90%)
  local copies, waits for them, and re-layouts  1.86 us (7%)
  between operations  0.65 us (2%)
    pallas_call x1, Pallas kernels, body(): pl.pallas_call(functools.partial(kernel, rows, cols), out_shape=(jax.Shap...  25.3 us
    unnamed x4, local copies, waits for them, and re-layouts  1.86 us

profile of v2, /device:TPU:1, one launch (start us, length us, event | category | flops | bytes accessed | tf_op | source)
XLA Modules:
  0.0 27.8 jit_solution(13347554073716126136)
XLA Ops:
  0.6 25.3 %shard_map.68 = (f32[1,1024]{1,0:T(1,128)}, f32[1,1024]{1,0:T(1,128)}) custom-call(s32[4,1,1024]{2,1,0:T(1,128)} %boxes_hbm.1, s32[4,1,1024]{2,1,0:T(1,128)} %boxes_hbm.1, s32[1,8]{1,0:T(1,128)} %counts_hbm.1, s32[1,8]{1,0:T(1,128)} %tails_hbm.1, f32[1,1024]{1,0:T(1,128)} %doses_hbm.1, f32[512,512]{1,0:T(8,128)} %gain_hbm.1), custom_call_target="tpu_custom_call" | custom-call | tf_op jit(solution)/shard_map/pallas_call | solution.py:321
  25.9 0.0 copy-start
  25.9 1.3 %copy.9 = f32[1,1024]{1,0:T(1,128)} copy(f32[1,1024]{1,0:T(1,128)} %get-tuple-element.4) | data formatting | bytes 8192
  27.2 0.0 copy-done
  27.2 0.6 %copy.10 = f32[1,1024]{1,0:T(1,128)} copy(f32[1,1024]{1,0:T(1,128)S(1)} %copy-done) | data formatting | bytes 8192
Async XLA Ops:
  25.9 1.3 %copy-start = (f32[1,1024]{1,0:T(1,128)S(1)}, f32[1,1024]{1,0:T(1,128)}, u32[]{:S(2)}) copy-start(f32[1,1024]{1,0:T(1,128)} %get-tuple-element.5) | copy-start | bytes 12292

commit v3 on v2

--- a/solution.py
+++ b/solution.py
@@ -16,6 +16,7 @@
 LANES = 128
 EDGE_STEP = 16
 UNROLL = 16
+STEP = 128
 
 FORWARD_RANGE = 4.0
 BACK_RATIO = 0.75
@@ -232,39 +233,35 @@
     def total_of(sums):
         return flat((sums[0] + sums[1]) + (sums[2] + sums[3]))
 
-    def build(g, sums):
-        sums = list(sums)
-        kept = []
-        for n in range(UNROLL):
-            j = g * UNROLL + n
-            low_x, low_y, high_x, high_y = (box_scalar[k, 0, j] for k in range(4))
-            kept.append((edge_x[low_x] - edge_x[high_x]) * (edge_y[low_y] - edge_y[high_y]))
-        for n in range(UNROLL):
-            j = g * UNROLL + n
-            pairs[j] = kept[n]
-            sums[n % 4] += kept[n] * dose_wide[pl.ds(j, 1), :]
-        return tuple(sums)
-
-    widen(dose)
-    forward = total_of(lax.fori_loop(0, slots // UNROLL, build, zero))
-
     fetch.wait()
     high, low = halves(gain[...])
     gain2[:, 0:tile] = high
     gain2[:, tile:2 * tile] = low
-    step = 256
-
-    def sample(i, _):
-        at = pl.ds(pl.multiple_of(i * step, step), step)
+    step = STEP
+
+    def build(g, sums):
+        at = pl.ds(pl.multiple_of(g * step, step), step)
         mid_x = (boxes[0, :, at] + boxes[2, :, at]) >> 1
         mid_y = (boxes[1, :, at] + boxes[3, :, at]) >> 1
         pixel = lax.broadcasted_iota(jnp.int32, (tile, step), 0)
         hot = jnp.where(pixel == mid_x, 1.0, 0.0).astype(jnp.bfloat16)
         taken = mxu(gain2[...], jnp.concatenate([hot, hot], axis=0))
         sens[:, at] = jnp.sum(jnp.where(pixel == mid_y, taken, 0.0), axis=0, keepdims=True)
-        return 0
-
-    lax.fori_loop(0, slots // step, sample, 0)
+        sums = list(sums)
+        for first in range(0, step, UNROLL):
+            kept = []
+            for n in range(first, first + UNROLL):
+                j = g * step + n
+                low_x, low_y, high_x, high_y = (box_scalar[k, 0, j] for k in range(4))
+                kept.append((edge_x[low_x] - edge_x[high_x]) * (edge_y[low_y] - edge_y[high_y]))
+            for n in range(first, first + UNROLL):
+                j = g * step + n
+                pairs[j] = kept[n - first]
+                sums[n % 4] += kept[n - first] * dose_wide[pl.ds(j, 1), :]
+        return tuple(sums)
+
+    widen(dose)
+    forward = total_of(lax.fori_loop(0, slots // step, build, zero))
 
     for k in range(ITERS):
         if k:

time: 28.1 us -> 26.4 us (0.940)
  Pallas kernels: 25.3 us -> 23.6 us
    pallas_call x1, Pallas kernels: 25.3 us -> 23.6 us  [body(): pl.pallas_call(functools.partial(kernel, rows, cols), out_shape=(jax.Shap...]
where the time goes in v3:
time: 26.4 us; the launch traced here: 26.1 us
  Pallas kernels  23.6 us (89%)
  local copies, waits for them, and re-layouts  1.86 us (7%)
  between operations  0.65 us (2%)
    pallas_call x1, Pallas kernels, body(): pl.pallas_call(functools.partial(kernel, rows, cols), out_shape=(jax.Shap...  23.6 us
    unnamed x4, local copies, waits for them, and re-layouts  1.86 us

profile of v3, /device:TPU:1, one launch (start us, length us, event | category | flops | bytes accessed | tf_op | source)
XLA Modules:
  0.0 26.1 jit_solution(13399056089158529607)
XLA Ops:
  0.6 23.6 %shard_map.68 = (f32[1,1024]{1,0:T(1,128)}, f32[1,1024]{1,0:T(1,128)}) custom-call(s32[4,1,1024]{2,1,0:T(1,128)} %boxes_hbm.1, s32[4,1,1024]{2,1,0:T(1,128)} %boxes_hbm.1, s32[1,8]{1,0:T(1,128)} %counts_hbm.1, s32[1,8]{1,0:T(1,128)} %tails_hbm.1, f32[1,1024]{1,0:T(1,128)} %doses_hbm.1, f32[512,512]{1,0:T(8,128)} %gain_hbm.1), custom_call_target="tpu_custom_call" | custom-call | tf_op jit(solution)/shard_map/pallas_call | solution.py:318
  24.2 0.0 copy-start
  24.2 1.3 %copy.9 = f32[1,1024]{1,0:T(1,128)} copy(f32[1,1024]{1,0:T(1,128)} %get-tuple-element.4) | data formatting | bytes 8192
  25.5 0.0 copy-done
  25.5 0.6 %copy.10 = f32[1,1024]{1,0:T(1,128)} copy(f32[1,1024]{1,0:T(1,128)S(1)} %copy-done) | data formatting | bytes 8192
Async XLA Ops:
  24.2 1.3 %copy-start = (f32[1,1024]{1,0:T(1,128)S(1)}, f32[1,1024]{1,0:T(1,128)}, u32[]{:S(2)}) copy-start(f32[1,1024]{1,0:T(1,128)} %get-tuple-element.5) | copy-start | bytes 12292

commit v4 on v3

--- a/solution.py
+++ b/solution.py
@@ -49,8 +49,8 @@
 
 def kernel(
     rows, cols,
-    box_scalar, boxes_hbm, counts_hbm, tails_hbm, doses_hbm, gain_hbm, dose_out, exposure_out,
-    boxes, counts, tails, doses, near_x, near_y, edge_x, edge_y, dose_wide,
+    boxes_hbm, counts_hbm, tails_hbm, doses_hbm, gain_hbm, dose_out, exposure_out,
+    boxes, counts, tails, doses, box_scalar, near_x, near_y, edge_x, edge_y, dose_wide,
     gain, gain2, pairs, column, down_t, side_t, across, downward,
     wx2, wy2, wy_own, wy_halo, wx_halo, sens,
     coarse, coarse_t, corner_out, halo_y, halo_x, corner_in,
@@ -82,13 +82,14 @@
         pltpu.make_async_copy(src, dst, in_sem.at[n])
         for n, (src, dst) in enumerate((
             (boxes_hbm, boxes), (counts_hbm, counts), (tails_hbm, tails), (doses_hbm, doses),
-            (gain_hbm, gain),
+            (gain_hbm, gain), (boxes_hbm, box_scalar),
         ))
     ]
-    fetch = fetches[4]
+    fetch, fetch_scalar = fetches[4:]
     for one in fetches[:4]:
         one.start()
     fetch.start()
+    fetch_scalar.start()
     for one in fetches[:4]:
         one.wait()
 
@@ -234,6 +235,7 @@
         return flat((sums[0] + sums[1]) + (sums[2] + sums[3]))
 
     fetch.wait()
+    fetch_scalar.wait()
     high, low = halves(gain[...])
     gain2[:, 0:tile] = high
     gain2[:, tile:2 * tile] = low
@@ -318,14 +320,14 @@
     return pl.pallas_call(
         functools.partial(kernel, rows, cols),
         out_shape=(jax.ShapeDtypeStruct((1, slots), f32),) * 2,
-        in_specs=[pl.BlockSpec(memory_space=pltpu.SMEM)]
-        + [pl.BlockSpec(memory_space=pltpu.HBM)] * 5,
+        in_specs=[pl.BlockSpec(memory_space=pltpu.HBM)] * 5,
         out_specs=(vmem, vmem),
         scratch_shapes=[
             pltpu.VMEM(shot_boxes.shape, jnp.int32),
             pltpu.VMEM(block_counts.shape, jnp.int32),
             pltpu.VMEM(tail_shots.shape, jnp.int32),
             pltpu.VMEM(doses.shape, f32),
+            pltpu.SMEM(shot_boxes.shape, jnp.int32),
             pltpu.VMEM((3 * EDGE_STEP, slots // LANES, LANES), f32),
             pltpu.VMEM((3 * EDGE_STEP, slots // LANES, LANES), f32),
             pltpu.VMEM((tile + EDGE_STEP, slots // LANES, LANES), f32),
@@ -351,14 +353,14 @@
             pltpu.VMEM((ITERS, 2 * REACH, cg), f32),
             pltpu.VMEM((ITERS, 2 * REACH, cg), f32),
             pltpu.VMEM((ITERS, 4, 8, LANES), f32),
-            pltpu.SemaphoreType.DMA((5,)),
+            pltpu.SemaphoreType.DMA((6,)),
             pltpu.SemaphoreType.DMA((ITERS, 8)),
             pltpu.SemaphoreType.DMA((ITERS, 8)),
         ],
         compiler_params=pltpu.CompilerParams(
             collective_id=0, has_side_effects=True, vmem_limit_bytes=60 * 1024 * 1024
         ),
-    )(shot_boxes, shot_boxes, block_counts, tail_shots, doses, pixel_gain)
+    )(shot_boxes, block_counts, tail_shots, doses, pixel_gain)
 
 
 def solution(mesh):

time: 26.4 us -> 25.4 us (0.962)
  Pallas kernels: 23.6 us -> 22.6 us
    pallas_call x1, Pallas kernels: 23.6 us -> 22.6 us  [body(): pl.pallas_call(functools.partial(kernel, rows, cols), out_shape=(jax.Shap...]
where the time goes in v4:
time: 25.4 us; the launch traced here: 25.1 us
  Pallas kernels  22.6 us (89%)
  local copies, waits for them, and re-layouts  1.86 us (7%)
  between operations  0.65 us (3%)
    pallas_call x1, Pallas kernels, body(): pl.pallas_call(functools.partial(kernel, rows, cols), out_shape=(jax.Shap...  22.6 us
    unnamed x4, local copies, waits for them, and re-layouts  1.86 us

profile of v4, /device:TPU:1, one launch (start us, length us, event | category | flops | bytes accessed | tf_op | source)
XLA Modules:
  0.0 25.1 jit_solution(11467310992865664829)
XLA Ops:
  0.6 22.6 %shard_map.68 = (f32[1,1024]{1,0:T(1,128)}, f32[1,1024]{1,0:T(1,128)}) custom-call(s32[4,1,1024]{2,1,0:T(1,128)} %boxes_hbm.1, s32[1,8]{1,0:T(1,128)} %counts_hbm.1, s32[1,8]{1,0:T(1,128)} %tails_hbm.1, f32[1,1024]{1,0:T(1,128)} %doses_hbm.1, f32[512,512]{1,0:T(8,128)} %gain_hbm.1), custom_call_target="tpu_custom_call" | custom-call | tf_op jit(solution)/shard_map/pallas_call | solution.py:320
  23.3 0.0 copy-start
  23.3 1.3 %copy.9 = f32[1,1024]{1,0:T(1,128)} copy(f32[1,1024]{1,0:T(1,128)} %get-tuple-element.4) | data formatting | bytes 8192
  24.5 0.0 copy-done
  24.5 0.6 %copy.10 = f32[1,1024]{1,0:T(1,128)} copy(f32[1,1024]{1,0:T(1,128)S(1)} %copy-done) | data formatting | bytes 8192
Async XLA Ops:
  23.3 1.3 %copy-start = (f32[1,1024]{1,0:T(1,128)S(1)}, f32[1,1024]{1,0:T(1,128)}, u32[]{:S(2)}) copy-start(f32[1,1024]{1,0:T(1,128)} %get-tuple-element.5) | copy-start | bytes 12292
